TPU v7x, 32 devices: a whole 2x2x4 slice. The times are simulated.
32 devices in a mesh: ulysses: 2 (over x), context: 16 (over z, y, core).
Axes of the slice: x: 2, y: 2, z: 4, core: 2. Of those that a mesh axis runs over, the one named last changes fastest.
Arguments:
- queries: bfloat16 [3072, 5120], P(('context', 'ulysses')), may hold values from -7 to 7
- key_vectors: bfloat16 [3072, 5120], P(('context', 'ulysses')), may hold values from -7 to 7
- value_vectors: bfloat16 [3072, 5120], P(('context', 'ulysses')), may hold values from -6 to 6
- labels: int32 [40], replicated, may hold values from 0 to 1, as said below
- block_lists: int32 [40, 48, 5], replicated, may hold values from 0 to 47, as said below
- counts: int32 [40, 48], replicated, may hold values from 1 to 5, as said below
- query_scale: float32 [40], replicated, may hold values from 1.5 to 3
- key_scale: float32 [40], replicated, may hold values from 1.5 to 3
- value_scale: float32 [40], replicated, may hold values from 0.5 to 2
Outputs:
- attended: bfloat16 [3072, 5120], P(('context', 'ulysses'))
Inputs may be any that keep to these rules, and one draw needn't show every extreme that they name: `labels`: exactly 16 entries are 1, the others 0; every aligned run of 20 heads holds at least one 0. Every entry of block_lists[h, b] lies within 2 blocks of b; the first entry is b itself and the first counts[h, b] entries are distinct. counts[h, b] is at least one less than and at most the number of blocks of the clip within 2 blocks of b; every head has a query block that uses all 5 entries.
All inputs are finite; a program needn't handle non-finite values.
Results may differ from a plain program's by a relative error of at most 0.0024.
Values may be sent and summed in bfloat16 or wider, within the bound.
A program may use at most 128 MiB of HBM per device.

v0:
```python
import math

import jax
import jax.numpy as jnp
from jax import lax
from jax.sharding import PartitionSpec as P

FRAMES = 16
MARGIN = 2
BLOCK = 64


def padded(cells, sides, width, closed):
    for axis, dim in sides:
        count = lax.axis_size(axis)
        ends = count if closed else count - 1
        head = lax.slice_in_dim(cells, 0, width, axis=dim)
        tail = lax.slice_in_dim(cells, cells.shape[dim] - width, cells.shape[dim], axis=dim)
        cells = jnp.concatenate(
            [
                lax.ppermute(tail, axis, [(i, (i + 1) % count) for i in range(ends)]),
                cells,
                lax.ppermute(head, axis, [((i + 1) % count, i) for i in range(ends)]),
            ],
            axis=dim,
        )
    return cells


def attend_heads(
    query_rows,
    extended,
    head_ids,
    block_ids,
    anchors,
    block_lists,
    counts,
    query_scale,
    key_scale,
    value_scale,
):
    rows, heads_here, head_width = query_rows.shape
    blocks = rows // BLOCK
    list_length = block_lists.shape[2]
    logit_scale = (
        jnp.take(query_scale, head_ids) * jnp.take(key_scale, head_ids) / math.sqrt(head_width)
    )
    value_factor = jnp.take(value_scale, head_ids)

    def one_head(head_index):
        head = lax.dynamic_index_in_dim(head_ids, head_index, 0, keepdims=False)
        query_tiles = lax.dynamic_index_in_dim(query_rows, head_index, 1, keepdims=False).reshape(
            blocks, BLOCK, head_width
        )
        key_column = lax.dynamic_index_in_dim(extended, head_index, 1, keepdims=False).reshape(
            -1, BLOCK, head_width
        )
        value_column = lax.dynamic_index_in_dim(
            extended, head_index + heads_here, 1, keepdims=False
        ).reshape(-1, BLOCK, head_width)
        global_ids = lax.dynamic_index_in_dim(block_ids, head_index, 0, keepdims=False)
        anchor = lax.dynamic_index_in_dim(anchors, head_index, 0, keepdims=False)
        head_lists = jnp.take(
            lax.dynamic_index_in_dim(block_lists, head, 0, keepdims=False), global_ids, axis=0
        )
        allowed = jnp.take(
            lax.dynamic_index_in_dim(counts, head, 0, keepdims=False), global_ids, axis=0
        )
        chosen = anchor[:, None] + head_lists - global_ids[:, None]
        collected_keys = key_column[chosen].reshape(blocks, list_length * BLOCK, head_width)
        collected_values = value_column[chosen].reshape(blocks, list_length * BLOCK, head_width)
        attention_logits = (
            jnp.einsum(
                "fac,foc->fao", query_tiles, collected_keys, preferred_element_type=jnp.float32
            )
            * logit_scale[head_index]
        )
        valid = jnp.repeat(jnp.arange(list_length)[None, :] < allowed[:, None], BLOCK, axis=1)
        attention_logits = jnp.where(valid[:, None, :], attention_logits, -jnp.inf)
        peak = jnp.max(attention_logits, axis=-1, keepdims=True)
        weight = jnp.exp(attention_logits - peak)
        total = jnp.sum(weight, axis=-1, keepdims=True)
        blended_output = jnp.einsum(
            "oem,omg->oeg",
            weight.astype(jnp.bfloat16),
            collected_values,
            preferred_element_type=jnp.float32,
        )
        output = (blended_output * (value_factor[head_index] / total)).astype(jnp.bfloat16)
        return output.reshape(rows, head_width)

    result = lax.map(one_head, jnp.arange(heads_here, dtype=jnp.int32))
    return jnp.transpose(result, (1, 0, 2))


def block_maps(context_index, context, spans, run_blocks):
    local = jnp.arange(spans * run_blocks, dtype=jnp.int32)
    run = local // run_blocks
    inner = local % run_blocks
    line_ids = (run * context + context_index) * run_blocks + inner
    line_anchor = run * (run_blocks + 2 * MARGIN) + inner + MARGIN
    frame_ids = context_index * (spans * run_blocks) + local
    frame_anchor = local + MARGIN
    return (line_ids, line_anchor, frame_ids, frame_anchor)


def into_pieces(rows_array, context):
    rows, heads_here, head_width = rows_array.shape
    return rows_array.reshape(context, rows // context, heads_here, head_width)


def into_lines(moved, spans):
    context, piece, heads_here, head_width = moved.shape
    frames = context // spans
    lines = moved.reshape(frames, spans, piece, heads_here, head_width).transpose(1, 2, 0, 3, 4)
    return lines.reshape(spans, piece * frames, heads_here, head_width)


def out_of_lines(line_rows, context, spans):
    rows, heads_here, head_width = line_rows.shape
    piece = rows // context
    frames = context // spans
    pieces = line_rows.reshape(spans, piece, frames, heads_here, head_width).transpose(
        2, 0, 1, 3, 4
    )
    return pieces.reshape(context, piece, heads_here, head_width)


def line_rims(line_joined):
    width = MARGIN * BLOCK
    extended = padded(line_joined, (("context", 1),), MARGIN * BLOCK, True)
    context_index = lax.axis_index("context")
    last_index = lax.axis_size("context") - 1
    lower = extended[:, :width]
    middle = extended[:, width:-width]
    upper = extended[:, -width:]
    lower_moved = jnp.concatenate([jnp.zeros_like(lower[:1]), lower[:-1]], axis=0)
    upper_moved = jnp.concatenate([upper[1:], jnp.zeros_like(upper[:1])], axis=0)
    lower = jnp.where(context_index == 0, lower_moved, lower)
    upper = jnp.where(context_index == last_index, upper_moved, upper)
    joined = jnp.concatenate([lower, middle, upper], axis=1)
    return joined.reshape(-1, joined.shape[2], joined.shape[3])


def frame_rims(frame_joined):
    return padded(frame_joined, (("context", 0),), MARGIN * BLOCK, False)


def shards(
    queries,
    key_vectors,
    value_vectors,
    labels,
    block_lists,
    counts,
    query_scale,
    key_scale,
    value_scale,
):
    groups = lax.axis_size("ulysses")
    context = lax.axis_size("context")
    tokens_here = queries.shape[0]
    head_count = labels.shape[0]
    head_width = queries.shape[1] // head_count
    per_group = head_count // groups
    shard_rows = tokens_here * groups
    spans = context // FRAMES
    piece = shard_rows // context
    run_blocks = piece * FRAMES // BLOCK
    group_index = lax.axis_index("ulysses")
    context_index = lax.axis_index("context")
    line_ids, line_anchor, frame_ids, frame_anchor = block_maps(
        context_index, context, spans, run_blocks
    )
    split_queries = queries.reshape(tokens_here, head_count, head_width)
    split_keys = key_vectors.reshape(tokens_here, head_count, head_width)
    split_values = value_vectors.reshape(tokens_here, head_count, head_width)
    grouped_queries = split_queries.reshape(tokens_here, groups, per_group, head_width)
    grouped_keys = split_keys.reshape(tokens_here, groups, per_group, head_width)
    grouped_values = split_values.reshape(tokens_here, groups, per_group, head_width)
    frame_queries, frame_keys, frame_values = (
        lax.all_to_all(grouped_queries, "ulysses", split_axis=1, concat_axis=0, tiled=True),
        lax.all_to_all(grouped_keys, "ulysses", split_axis=1, concat_axis=0, tiled=True),
        lax.all_to_all(grouped_values, "ulysses", split_axis=1, concat_axis=0, tiled=True),
    )
    frame_queries = frame_queries.reshape(shard_rows, per_group, head_width)
    frame_keys = frame_keys.reshape(shard_rows, per_group, head_width)
    frame_values = frame_values.reshape(shard_rows, per_group, head_width)
    moved_queries, moved_keys, moved_values = (
        lax.all_to_all(
            into_pieces(frame_queries, context), "context", split_axis=0, concat_axis=0, tiled=True
        ),
        lax.all_to_all(
            into_pieces(frame_keys, context), "context", split_axis=0, concat_axis=0, tiled=True
        ),
        lax.all_to_all(
            into_pieces(frame_values, context), "context", split_axis=0, concat_axis=0, tiled=True
        ),
    )
    head_ids = group_index * per_group + jnp.arange(per_group, dtype=jnp.int32)
    temporal = jnp.take(labels, head_ids) == 1
    line_query = into_lines(moved_queries, spans).reshape(shard_rows, per_group, head_width)
    line_ext = line_rims(
        jnp.concatenate([into_lines(moved_keys, spans), into_lines(moved_values, spans)], axis=2)
    )
    frame_ext = frame_rims(jnp.concatenate([frame_keys, frame_values], axis=1))
    extra = line_ext.shape[0] - frame_ext.shape[0]
    frame_ext = jnp.pad(frame_ext, ((0, extra), (0, 0), (0, 0)))
    doubled = jnp.concatenate([temporal, temporal])
    query_rows = jnp.where(temporal[None, :, None], line_query, frame_queries)
    extended = jnp.where(doubled[None, :, None], line_ext, frame_ext)
    block_ids = jnp.where(temporal[:, None], line_ids[None, :], frame_ids[None, :])
    anchors = jnp.where(temporal[:, None], line_anchor[None, :], frame_anchor[None, :])
    outputs = attend_heads(
        query_rows,
        extended,
        head_ids,
        block_ids,
        anchors,
        block_lists,
        counts,
        query_scale,
        key_scale,
        value_scale,
    )
    returned = lax.all_to_all(
        out_of_lines(outputs, context, spans), "context", split_axis=0, concat_axis=0, tiled=True
    )
    returned = returned.reshape(shard_rows, per_group, head_width)
    frame_outputs = jnp.where(temporal[None, :, None], returned, outputs)
    merged = lax.all_to_all(
        frame_outputs.reshape(shard_rows, 1, per_group, head_width),
        "ulysses",
        split_axis=0,
        concat_axis=1,
        tiled=True,
    )
    return merged.reshape(tokens_here, head_count * head_width)


def solution(mesh):
    placed = (
        P(("context", "ulysses"), None),
        P(("context", "ulysses"), None),
        P(("context", "ulysses"), None),
        P(),
        P(),
        P(),
        P(),
        P(),
        P(),
    )
    return jax.shard_map(
        shards,
        mesh=mesh,
        in_specs=placed,
        out_specs=P(("context", "ulysses"), None),
        check_vma=False,
    )
```

profile of v0, /device:TPU:0, one launch (start us, length us, event | category | flops | bytes accessed | tf_op | source)
XLA Modules:
  0.0 595.6 jit_solution(9574930149500055878)
XLA Ops:
  0.0 1.7 reshape_reshape.24
  2.9 4.2 all-to-all-start.2
  7.1 1.7 reshape_reshape.26
  10.0 10.8 %all-to-all-done.2 = bf16[96,2,20,128]{3,0,2,1:T(8,128)(2,1)S(1)} async-done(((bf16[96,2,20,128]{3,0,2,1:T(8,128)(2,1)}), bf16[96,2,20,128]{3,0,2,1:T(8,128)(2,1)S(1)}, u32[]{:S(2)}, u32[]{:S(2)}) %all-to-all-start.2) | async-done | bytes 983072 | tf_op jit(solution)/shard_map/all_to_all | solution.py:183
  20.8 4.4 all-to-all-start.4
  25.2 1.7 reshape_reshape.21
  28.1 9.8 %all-to-all-done.4 = bf16[96,2,20,128]{3,0,2,1:T(8,128)(2,1)} async-done(((bf16[96,2,20,128]{3,0,2,1:T(8,128)(2,1)}), bf16[96,2,20,128]{3,0,2,1:T(8,128)(2,1)}, u32[]{:S(2)}, u32[]{:S(2)}) %all-to-all-start.4) | async-done | bytes 983072 | tf_op jit(solution)/shard_map/all_to_all | solution.py:184
  37.9 3.6 all-to-all-start
  41.6 1.7 copy.55
  43.3 9.9 %all-to-all-done = bf16[96,2,20,128]{3,0,2,1:T(8,128)(2,1)S(1)} async-done(((bf16[96,2,20,128]{3,0,2,1:T(8,128)(2,1)}), bf16[96,2,20,128]{3,0,2,1:T(8,128)(2,1)S(1)}, u32[]{:S(2)}, u32[]{:S(2)}) %all-to-all-start) | async-done | bytes 983072 | tf_op jit(solution)/shard_map/all_to_all | solution.py:182
  54.1 5.6 all-to-all-start.3
  61.0 1.7 copy.59
  62.7 22.1 %all-to-all-done.3 = bf16[16,12,20,128]{3,2,1,0:T(8,128)(2,1)S(1)} async-done(((bf16[16,12,20,128]{3,2,1,0:T(8,128)(2,1)}), bf16[16,12,20,128]{3,2,1,0:T(8,128)(2,1)S(1)}, u32[]{:S(2)}, u32[]{:S(2)}) %all-to-all-start.3) | async-done | bytes 983072 | tf_op jit(solution)/shard_map/all_to_all | solution.py:193
  84.8 7.5 %all-to-all-start.5 = ((bf16[16,12,20,128]{3,2,1,0:T(8,128)(2,1)}), bf16[16,12,20,128]{3,2,1,0:T(8,128)(2,1)}, u32[]{:S(2)}, u32[]{:S(2)}) async-start(bf16[16,12,20,128]{3,2,1,0:T(8,128)(2,1)} %bitcast.154), calls=%async_computation.5 | async-start | bytes 2359296 | tf_op jit(solution)/shard_map/all_to_all | solution.py:196
  93.7 1.7 copy.51
  95.4 22.2 %all-to-all-done.5 = bf16[16,12,20,128]{3,2,1,0:T(8,128)(2,1)} async-done(((bf16[16,12,20,128]{3,2,1,0:T(8,128)(2,1)}), bf16[16,12,20,128]{3,2,1,0:T(8,128)(2,1)}, u32[]{:S(2)}, u32[]{:S(2)}) %all-to-all-start.5) | async-done | bytes 983072 | tf_op jit(solution)/shard_map/all_to_all | solution.py:196
  117.5 7.5 %all-to-all-start.1 = ((bf16[16,12,20,128]{3,2,1,0:T(8,128)(2,1)}), bf16[16,12,20,128]{3,2,1,0:T(8,128)(2,1)}, u32[]{:S(2)}, u32[]{:S(2)}) async-start(bf16[16,12,20,128]{3,2,1,0:T(8,128)(2,1)} %bitcast.152), calls=%async_computation.1 | async-start | bytes 2359296 | tf_op jit(solution)/shard_map/all_to_all | solution.py:190
  125.1 1.7 copy.56
  126.8 2.0 copy.60
  128.8 1.8 fusion.14
  130.6 4.4 collective-permute-start.1
  138.0 1.8 fusion.13
  139.8 2.4 collective-permute-start.2
  142.2 1.5 collective-permute-start.3
  143.7 20.7 %all-to-all-done.1 = bf16[16,12,20,128]{3,2,1,0:T(8,128)(2,1)} async-done(((bf16[16,12,20,128]{3,2,1,0:T(8,128)(2,1)}), bf16[16,12,20,128]{3,2,1,0:T(8,128)(2,1)}, u32[]{:S(2)}, u32[]{:S(2)}) %all-to-all-start.1) | async-done | bytes 983072 | tf_op jit(solution)/shard_map/all_to_all | solution.py:190
  164.4 1.7 copy.52
  167.2 1.4 broadcast_select_fusion.1
  170.1 12.4 %fusion.12 = bf16[448,40,128]{2,0,1:T(8,128)(2,1)} fusion(bf16[1,128,40,128]{3,1,2,0:T(8,128)(2,1)S(1)} %broadcast_select_fusion.1, bf16[1,192,20,128]{3,1,2,0:T(8,128)(2,1)S(1)} %bitcast.149, bf16[1,192,20,128]{3,1,2,0:T(8,128)(2,1)S(1)} %bitcast.147, bf16[1,128,40,128]{3,1,2,0:T(8,128)(2,1)S(1)} %broadcast_select_fusion.2, ...), kind=kLoop, calls=%fused_computation.41 | loop fusion | flops 38993920 | bytes 13762600 | tf_op jit(solution)/shard_map/jit(_where)/select_n | solution.py:211
  182.5 328.6 %while.12 = (s32[]{:T(128)}, bf16[20,192,128]{2,1,0:T(8,128)(2,1)S(1)}, s32[20]{0:T(128)S(1)}, s32[20,3]{1,0:T(8,128)S(1)}, s32[20]{0:T(128)S(1)}, /*index=5*/s3...) while((s32[]{:T(128)}, ...), condition=%wide.region_3.5_spmd, body=%wide.region_0.4_spmd.sunk | while | flops 31938516 | bytes 2988280 | solution.py:92
  511.8 63.1 %all_to_all.80 = bf16[16,12,20,128]{3,2,1,0:T(8,128)(2,1)S(1)} all-to-all(bf16[16,12,20,128]{3,2,1,0:T(8,128)(2,1)S(1)} %bitcast.159), channel_id=1, replica_groups=mesh['ulysses'=2,'context'=16] {'context'}, dimensions={0} | all-to-all | bytes 1966080 | tf_op jit(solution)/shard_map/all_to_all | solution.py:226
  575.8 18.2 %all_to_all.81 = bf16[192,1,20,128]{3,2,1,0:T(8,128)(2,1)S(1)} all-to-all(bf16[192,1,20,128]{3,2,1,0:T(8,128)(2,1)S(1)} %copy.64), channel_id=1, replica_groups=mesh['ulysses'=2,'context'=16] {'ulysses'}, dimensions={0} | all-to-all | bytes 1966080 | tf_op jit(solution)/shard_map/all_to_all | solution.py:231
  594.2 1.4 reshape.354
  (616 shorter events, 225.9 us)
Async XLA Ops:
  0.0 135.0 %copy-start = (f32[40]{0:T(128)S(1)}, f32[40]{0:T(128)}, u32[]{:S(2)}) copy-start(f32[40]{0:T(128)} %param.21) | copy-start | bytes 484
  2.9 17.9 %all-to-all-start.2 = ((bf16[96,2,20,128]{3,0,2,1:T(8,128)(2,1)}), bf16[96,2,20,128]{3,0,2,1:T(8,128)(2,1)S(1)}, u32[]{:S(2)}, u32[]{:S(2)}) async-start(bf16[96,2,20,128]{3,0,2,1:T(8,128)(2,1)} %copy.53), calls=%async_computation.2 | async-start | bytes 1966080 | tf_op jit(solution)/shard_map/all_to_all | solution.py:183
  20.8 17.1 %all-to-all-start.4 = ((bf16[96,2,20,128]{3,0,2,1:T(8,128)(2,1)}), bf16[96,2,20,128]{3,0,2,1:T(8,128)(2,1)}, u32[]{:S(2)}, u32[]{:S(2)}) async-start(bf16[96,2,20,128]{3,0,2,1:T(8,128)(2,1)} %copy.57), calls=%async_computation.4 | async-start | bytes 1966080 | tf_op jit(solution)/shard_map/all_to_all | solution.py:184
  37.9 15.3 %all-to-all-start = ((bf16[96,2,20,128]{3,0,2,1:T(8,128)(2,1)}), bf16[96,2,20,128]{3,0,2,1:T(8,128)(2,1)S(1)}, u32[]{:S(2)}, u32[]{:S(2)}) async-start(bf16[96,2,20,128]{3,0,2,1:T(8,128)(2,1)} %copy.49), calls=%async_computation | async-start | bytes 1966080 | tf_op jit(solution)/shard_map/all_to_all | solution.py:182
  53.2 0.9 copy-start.9
  54.1 30.7 %all-to-all-start.3 = ((bf16[16,12,20,128]{3,2,1,0:T(8,128)(2,1)}), bf16[16,12,20,128]{3,2,1,0:T(8,128)(2,1)S(1)}, u32[]{:S(2)}, u32[]{:S(2)}) async-start(bf16[16,12,20,128]{3,2,1,0:T(8,128)(2,1)} %bitcast.155), calls=%async_computation.3 | async-start | bytes 2359296 | tf_op jit(solution)/shard_map/all_to_all | solution.py:193
  84.8 7.5 %copy-start.8 = (bf16[16,12,20,128]{3,2,1,0:T(8,128)(2,1)}, bf16[16,12,20,128]{3,2,1,0:T(8,128)(2,1)S(1)}, u32[]{:S(2)}) copy-start(bf16[16,12,20,128]{3,2,1,0:T(8,128)(2,1)S(1)} %all-to-all-done.3) | copy-start | bytes 2949124
  84.8 32.7 %all-to-all-start.5 = ((bf16[16,12,20,128]{3,2,1,0:T(8,128)(2,1)}), bf16[16,12,20,128]{3,2,1,0:T(8,128)(2,1)}, u32[]{:S(2)}, u32[]{:S(2)}) async-start(bf16[16,12,20,128]{3,2,1,0:T(8,128)(2,1)} %bitcast.154), calls=%async_computation.5 | async-start | bytes 2359296 | tf_op jit(solution)/shard_map/all_to_all | solution.py:196
  117.5 46.9 %all-to-all-start.1 = ((bf16[16,12,20,128]{3,2,1,0:T(8,128)(2,1)}), bf16[16,12,20,128]{3,2,1,0:T(8,128)(2,1)}, u32[]{:S(2)}, u32[]{:S(2)}) async-start(bf16[16,12,20,128]{3,2,1,0:T(8,128)(2,1)} %bitcast.152), calls=%async_computation.1 | async-start | bytes 2359296 | tf_op jit(solution)/shard_map/all_to_all | solution.py:190
  126.8 3.8 copy-start.4
  128.8 1.8 copy-start.6
  128.8 6.9 %copy-start.1 = (f32[40]{0:T(128)S(1)}, f32[40]{0:T(128)}, u32[]{:S(2)}) copy-start(f32[40]{0:T(128)} %param.19) | copy-start | bytes 484
  130.6 5.8 copy-start.2
  130.6 6.5 %copy-start.3 = (s32[40]{0:T(128)S(1)}, s32[40]{0:T(128)}, u32[]{:S(2)}) copy-start(s32[40]{0:T(128)} %param.16) | copy-start | bytes 484
  130.6 36.5 %collective-permute-start.1 = (bf16[1,128,40,128]{3,1,2,0:T(8,128)(2,1)}, bf16[1,128,40,128]{3,1,2,0:T(8,128)(2,1)}, u32[]{:S(2)}, u32[]{:S(2)}) collective-permute-start(bf16[1,128,40,128]{3,1,2,0:T(8,128)(2,1)} %get-tuple-element.250), channel_id=1, source_target_pairs={{1,0},{2,1},{3,2},{4,3},{5,4},{6,5},{7,6},{8,7},{9,8},{10,9},{11,1... | collective-permute-start | bytes 3932168 | tf_op jit(solution)/shard_map/ppermute | solution.py:23
  137.9 30.7 %collective-permute-start = (bf16[1,128,40,128]{3,1,2,0:T(8,128)(2,1)}, bf16[1,128,40,128]{3,1,2,0:T(8,128)(2,1)}, u32[]{:S(2)}, u32[]{:S(2)}) collective-permute-start(bf16[1,128,40,128]{3,1,2,0:T(8,128)(2,1)} %get-tuple-element.249), channel_id=1, source_target_pairs={{0,1},{1,2},{2,3},{3,4},{4,5},{5,6},{6,7},{7,8},{8,9},{9,10},{10,1... | collective-permute-start | bytes 3932168 | tf_op jit(solution)/shard_map/ppermute | solution.py:21
  139.8 28.9 %collective-permute-start.2 = (bf16[128,40,128]{2,0,1:T(8,128)(2,1)}, bf16[128,40,128]{2,0,1:T(8,128)(2,1)}, u32[]{:S(2)}, u32[]{:S(2)}) collective-permute-start(bf16[128,40,128]{2,0,1:T(8,128)(2,1)} %get-tuple-element.247), channel_id=1, source_target_pairs={{0,1},{1,2},{2,3},{3,4},{4,5},{5,6},{6,7},{7,8},{8,9},{9,10},{10,1... | collective-permute-start | bytes 3932168 | tf_op jit(solution)/shard_map/ppermute | solution.py:21
  142.2 26.6 %collective-permute-start.3 = (bf16[128,40,128]{2,0,1:T(8,128)(2,1)}, bf16[128,40,128]{2,0,1:T(8,128)(2,1)}, u32[]{:S(2)}, u32[]{:S(2)}) collective-permute-start(bf16[128,40,128]{2,0,1:T(8,128)(2,1)} %get-tuple-element.248), channel_id=1, source_target_pairs={{1,0},{2,1},{3,2},{4,3},{5,4},{6,5},{7,6},{8,7},{9,8},{10,9},{11,1... | collective-permute-start | bytes 3932168 | tf_op jit(solution)/shard_map/ppermute | solution.py:23
  168.6 1.2 copy-start.5
  168.6 1.5 copy-start.7
  168.7 13.8 %copy-start.10 = (bf16[20,192,128]{2,1,0:T(8,128)(2,1)S(1)}, bf16[20,192,128]{2,1,0:T(8,128)(2,1)}, u32[]{:S(2)}) copy-start(bf16[20,192,128]{2,1,0:T(8,128)(2,1)} %custom-call.16) | copy-start | bytes 2949124
where the time goes:
time: 602 us; the launch traced here: 596 us
  local copies, waits for them, and re-layouts  197 us (33%)
  loops' own time  117 us (19%)
  waiting for transfers between devices  95.5 us (16%)
  blocking collectives  81.3 us (14%)
  starting transfers between devices  41 us (7%)
  other arithmetic  39.6 us (7%)
  matrix products  23.7 us (4%)
    another operation x1, loops' own time, attend_heads(): result = lax.map(one_head, jnp.arange(heads_here, dtype=jnp.int32))  117 us
    all_to_all x1, blocking collectives, shards(): lax.all_to_all(out_of_lines(outputs, context, spans), 'context', split_ax...  63.1 us
    all_to_all x1, waiting for transfers between devices, shards(): lax.all_to_all(into_pieces(frame_values, context), 'context', split_axis=...  22.2 us
    all_to_all x1, waiting for transfers between devices, shards(): lax.all_to_all(into_pieces(frame_keys, context), 'context', split_axis=0,...  22.1 us
    all_to_all x1, waiting for transfers between devices, shards(): lax.all_to_all(into_pieces(frame_queries, context), 'context', split_axis...  20.7 us
    dynamic_slice x20, local copies, waits for them, and re-layouts, one_head(): lax.dynamic_index_in_dim(extended, head_index, 1, keepdims=False)  19.5 us
    dot_general x20, matrix products, one_head(): jnp.einsum('fac,foc->fao', query_tiles, collected_keys, preferred_element...  18.5 us
    all_to_all x1, blocking collectives, shards(): lax.all_to_all(frame_outputs.reshape(shard_rows, 1, per_group, head_width...  18.2 us
  transfers between devices with their start and end apart: 10, of which 6 were waited for; matrix products, arithmetic and copies ran while one was open for 5% of the time, Pallas kernels for 0%

commit v1 on v0

v1 whole, which is shorter than its diff:
```python
import functools
import math

import jax
import jax.numpy as jnp
from jax import lax
from jax.experimental import pallas as pl
from jax.experimental.pallas import tpu as pltpu
from jax.sharding import PartitionSpec as P

FRAMES = 16
TEMPORAL = 16
MARGIN = 2
BLOCK = 64
WIDTH = 128
GROUP = 8
RIM = MARGIN * BLOCK
PAIR = 2 * BLOCK
WINDOW = PAIR + 2 * RIM
MASKED = -1e30


def pack(
    labels,
    query_scale,
    key_scale,
    value_scale,
    bits,
    q_ref,
    k_ref,
    v_ref,
    packed,
    place,
    sorted_bits,
    logit_scale,
    value_factor,
):
    heads = labels.shape[0]

    def one(head, spatial):
        temporal = labels[head]
        slot = jnp.where(temporal == 1, heads - TEMPORAL + head - spatial, spatial)
        place[head] = slot
        logit_scale[slot] = query_scale[head] * key_scale[head] * (1.0 / math.sqrt(WIDTH))
        value_factor[slot] = value_scale[head]
        sorted_bits[pl.ds(slot, 1), :] = bits[pl.ds(head, 1), :]
        columns = pl.ds(pl.multiple_of(head * WIDTH, WIDTH), WIDTH)
        packed[slot, :, 0:WIDTH] = q_ref[:, columns]
        packed[slot, :, WIDTH : 2 * WIDTH] = k_ref[:, columns]
        packed[slot, :, 2 * WIDTH : 3 * WIDTH] = v_ref[:, columns]
        return spatial + 1 - temporal

    lax.fori_loop(0, heads, one, 0)


def unpack(place, returned, out_ref):
    def one(head, carry):
        columns = pl.ds(pl.multiple_of(head * WIDTH, WIDTH), WIDTH)
        out_ref[:, columns] = returned[place[head]]
        return carry

    lax.fori_loop(0, place.shape[0], one, 0)


def kernel(
    devices,
    ulysses,
    bits,
    logit_scale,
    value_scale,
    packed,
    returned,
    near,
    frames,
    lines,
    near_out,
    line_out,
    frame_out,
    swap,
    near_send,
    near_recv,
    far_send,
    far_recv,
    rim_send,
    rim_recv,
    own_sem,
    near_back_send,
    near_back_recv,
    far_back_send,
    far_back_recv,
):
    heads, rows = packed.shape[:2]
    spatial = heads - TEMPORAL
    share = spatial // GROUP
    near_rows = GROUP * rows
    line_rows = FRAMES * rows
    per_frame = devices // FRAMES
    groups = devices // GROUP
    near_pairs = near_rows // PAIR
    line_pairs = line_rows // PAIR
    tile = 16
    strip = tile * FRAMES
    strips = rows // tile

    me = lax.axis_index("context") * ulysses + lax.axis_index("ulysses")
    slot = lax.rem(me, GROUP)
    base = me - slot
    group = lax.div(me, GROUP)
    frame = lax.div(me, per_frame)
    chunk = lax.rem(me, per_frame)

    def device(index):
        return (lax.rem(index, ulysses), lax.div(index, ulysses))

    def near_peer(step):
        return lax.rem(slot + step, GROUP)

    def far_peer(step):
        return lax.rem(frame + step, FRAMES)

    has_lower = group > 0
    has_upper = group < groups - 1
    line_lower = chunk > 0
    line_upper = chunk < per_frame - 1
    mesh_id = pl.DeviceIdType.MESH

    barrier = pltpu.get_barrier_semaphore()

    def greet(index):
        pl.semaphore_signal(barrier, inc=1, device_id=device(index), device_id_type=mesh_id)

    for step in range(1, GROUP):
        greet(base + near_peer(step))
    for step in range(1, FRAMES):
        greet(far_peer(step) * per_frame + chunk)
    for away in (GROUP, 1):
        greet(lax.rem(me + away, devices))
        greet(lax.rem(me + devices - away, devices))
    pl.semaphore_wait(barrier, GROUP - 1 + FRAMES - 1 + 4)

    def near_copy(peer, source):
        return pltpu.make_async_remote_copy(
            src_ref=packed.at[pl.ds(share * peer, share)],
            dst_ref=near.at[:, pl.ds(RIM + rows * source, rows), :],
            send_sem=near_send.at[peer],
            recv_sem=near_recv.at[source],
            device_id=device(base + peer),
            device_id_type=mesh_id,
        )

    def far_copy(peer, source):
        return pltpu.make_async_remote_copy(
            src_ref=packed.at[spatial + peer],
            dst_ref=frames.at[source],
            send_sem=far_send.at[peer],
            recv_sem=far_recv.at[source],
            device_id=device(peer * per_frame + chunk),
            device_id_type=mesh_id,
        )

    for step in range(1, FRAMES):
        far_copy(far_peer(step), frame).start()
        if step < GROUP:
            near_copy(near_peer(step), slot).start()
    own_near = pltpu.make_async_copy(
        packed.at[pl.ds(share * slot, share)],
        near.at[:, pl.ds(RIM + rows * slot, rows), :],
        own_sem.at[0],
    )
    own_far = pltpu.make_async_copy(packed.at[spatial + frame], frames.at[frame], own_sem.at[1])
    own_near.start()
    own_far.start()

    turned = lax.broadcasted_iota(jnp.int32, (strip, strip), 0)
    across = lax.broadcasted_iota(jnp.int32, (strip, strip), 1)
    swap[...] = jnp.where(
        across == lax.rem(turned, tile) * tile + lax.div(turned, tile), 1.0, 0.0
    ).astype(jnp.bfloat16)

    rim_lanes = pl.ds(WIDTH, 2 * WIDTH)

    @pl.when(jnp.logical_not(has_lower))
    def _():
        near[:, 0:RIM, :] = jnp.zeros((share, RIM, 3 * WIDTH), jnp.bfloat16)

    @pl.when(jnp.logical_not(has_upper))
    def _():
        near[:, RIM + near_rows :, :] = jnp.zeros((share, RIM, 3 * WIDTH), jnp.bfloat16)

    @pl.when(jnp.logical_not(line_lower))
    def _():
        lines[0:RIM, :] = jnp.zeros((RIM, 3 * WIDTH), jnp.bfloat16)

    @pl.when(jnp.logical_not(line_upper))
    def _():
        lines[RIM + line_rows :, :] = jnp.zeros((RIM, 3 * WIDTH), jnp.bfloat16)

    def rim_copy(which, peer):
        source = (near_rows, RIM, line_rows, RIM)[which]
        target = (0, RIM + near_rows, 0, RIM + line_rows)[which]
        if which < 2:
            src = near.at[:, pl.ds(source, RIM), rim_lanes]
            dst = near.at[:, pl.ds(target, RIM), rim_lanes]
        else:
            src = lines.at[pl.ds(source, RIM), rim_lanes]
            dst = lines.at[pl.ds(target, RIM), rim_lanes]
        return pltpu.make_async_remote_copy(
            src_ref=src,
            dst_ref=dst,
            send_sem=rim_send.at[which],
            recv_sem=rim_recv.at[which],
            device_id=device(peer),
            device_id_type=mesh_id,
        )

    rims = (
        (has_upper, me + GROUP, has_lower),
        (has_lower, me - GROUP, has_upper),
        (line_upper, me + 1, line_lower),
        (line_lower, me - 1, line_upper),
    )

    def send_rim(which):
        @pl.when(rims[which][0])
        def _():
            rim_copy(which, rims[which][1]).start()

    def await_rim(which):
        @pl.when(rims[which][2])
        def _():
            rim_copy(which, me).wait_recv()

    key_block = lax.div(lax.broadcasted_iota(jnp.int32, (1, WINDOW), 1), BLOCK)
    key_bit = jnp.left_shift(jnp.ones_like(key_block), key_block)

    def attend(queries, keys, values, head, block):
        lower = jnp.where((key_bit & bits[head, block]) != 0, 0.0, MASKED)
        upper = jnp.where((key_bit & (bits[head, block + 1] * 2)) != 0, 0.0, MASKED)
        bias = jnp.concatenate(
            [
                jnp.broadcast_to(lower, (BLOCK, WINDOW)),
                jnp.broadcast_to(upper, (BLOCK, WINDOW)),
            ],
            axis=0,
        )
        score = lax.dot_general(
            queries, keys, (((1,), (1,)), ((), ())), preferred_element_type=jnp.float32
        )
        score = score * logit_scale[head] + bias
        peak = jnp.max(score, axis=-1, keepdims=True)
        weight = jnp.exp(score - peak)
        total = jnp.sum(weight, axis=-1, keepdims=True)
        mixed = jnp.dot(
            weight.astype(jnp.bfloat16), values, preferred_element_type=jnp.float32
        )
        return (mixed * (value_scale[head] / total)).astype(jnp.bfloat16)

    def near_pair(i, pair):
        start = pl.multiple_of(pair * PAIR, PAIR)
        head = share * slot + i
        near_out[i, pl.ds(start, PAIR), :] = attend(
            near[i, pl.ds(start + RIM, PAIR), 0:WIDTH],
            near[i, pl.ds(start, WINDOW), WIDTH : 2 * WIDTH],
            near[i, pl.ds(start, WINDOW), 2 * WIDTH : 3 * WIDTH],
            head,
            group * (near_rows // BLOCK) + 2 * pair,
        )

    line_head = spatial + frame

    def line_pair(pair):
        start = pl.multiple_of(pair * PAIR, PAIR)
        line_out[pl.ds(start, PAIR), :] = attend(
            lines[pl.ds(start + RIM, PAIR), 0:WIDTH],
            lines[pl.ds(start, WINDOW), WIDTH : 2 * WIDTH],
            lines[pl.ds(start, WINDOW), 2 * WIDTH : 3 * WIDTH],
            line_head,
            chunk * (line_rows // BLOCK) + 2 * pair,
        )

    for step in range(1, GROUP):
        near_copy(near_peer(step), near_peer(step)).wait_recv()
    own_near.wait()
    send_rim(0)
    send_rim(1)

    def near_middle(n, carry):
        for i in range(share):
            near_pair(i, n + 1)
        return carry

    lax.fori_loop(0, near_pairs - 2, near_middle, 0)

    for step in range(1, FRAMES):
        far_copy(far_peer(step), far_peer(step)).wait_recv()
    own_far.wait()

    def turn(s, carry):
        piece = frames[:, pl.ds(pl.multiple_of(s * tile, tile), tile), :]
        lines[pl.ds(pl.multiple_of(RIM + s * strip, RIM), strip), :] = jnp.dot(
            swap[...], piece.reshape(strip, 3 * WIDTH), preferred_element_type=jnp.float32
        ).astype(jnp.bfloat16)
        return carry

    lax.fori_loop(0, strips, turn, 0)
    send_rim(2)
    send_rim(3)

    await_rim(0)
    await_rim(1)

    def near_edge(i, carry):
        near_pair(i, 0)
        near_pair(i, near_pairs - 1)
        return carry

    lax.fori_loop(0, share, near_edge, 0)

    def near_back(peer, source):
        return pltpu.make_async_remote_copy(
            src_ref=near_out.at[:, pl.ds(rows * peer, rows), :],
            dst_ref=returned.at[pl.ds(share * source, share)],
            send_sem=near_back_send.at[peer],
            recv_sem=near_back_recv.at[source],
            device_id=device(base + peer),
            device_id_type=mesh_id,
        )

    def far_back(peer, source):
        return pltpu.make_async_remote_copy(
            src_ref=frame_out.at[peer],
            dst_ref=returned.at[spatial + source],
            send_sem=far_back_send.at[peer],
            recv_sem=far_back_recv.at[source],
            device_id=device(peer * per_frame + chunk),
            device_id_type=mesh_id,
        )

    for step in range(1, GROUP):
        near_back(near_peer(step), slot).start()
    own_near_back = pltpu.make_async_copy(
        near_out.at[:, pl.ds(rows * slot, rows), :],
        returned.at[pl.ds(share * slot, share)],
        own_sem.at[2],
    )
    own_near_back.start()

    def line_middle(n, carry):
        line_pair(2 * n + 1)
        line_pair(2 * n + 2)
        return carry

    lax.fori_loop(0, (line_pairs - 2) // 2, line_middle, 0)
    await_rim(2)
    await_rim(3)
    line_pair(0)
    line_pair(line_pairs - 1)

    def turn_back(s, carry):
        piece = jnp.dot(
            swap[...],
            line_out[pl.ds(pl.multiple_of(s * strip, strip), strip), :],
            preferred_element_type=jnp.float32,
        ).astype(jnp.bfloat16)
        frame_out[:, pl.ds(pl.multiple_of(s * tile, tile), tile), :] = piece.reshape(
            FRAMES, tile, WIDTH
        )
        return carry

    lax.fori_loop(0, strips, turn_back, 0)
    for step in range(1, FRAMES):
        far_back(far_peer(step), frame).start()
    own_far_back = pltpu.make_async_copy(
        frame_out.at[frame], returned.at[spatial + frame], own_sem.at[3]
    )
    own_far_back.start()

    for step in range(1, GROUP):
        near_copy(near_peer(step), slot).wait_send()
        near_back(near_peer(step), slot).wait_send()
        near_back(near_peer(step), near_peer(step)).wait_recv()
    for which in range(4):

        @pl.when(rims[which][0])
        def _(which=which):
            rim_copy(which, rims[which][1]).wait_send()

    own_near_back.wait()
    for step in range(1, FRAMES):
        far_copy(far_peer(step), frame).wait_send()
        far_back(far_peer(step), frame).wait_send()
        far_back(far_peer(step), far_peer(step)).wait_recv()
    own_far_back.wait()


def shards(
    devices,
    queries,
    key_vectors,
    value_vectors,
    labels,
    block_lists,
    counts,
    query_scale,
    key_scale,
    value_scale,
):
    rows, width = queries.shape
    heads = labels.shape[0]
    blocks = counts.shape[1]
    spatial = heads - TEMPORAL
    share = spatial // GROUP
    ulysses = lax.axis_size("ulysses")

    entries = jnp.arange(block_lists.shape[2], dtype=jnp.int32)
    offsets = block_lists - jnp.arange(blocks, dtype=jnp.int32)[None, :, None] + MARGIN
    bits = jnp.sum(
        jnp.where(entries < counts[:, :, None], jnp.left_shift(1, offsets), 0), axis=2
    ).astype(jnp.int32)

    near_rows = GROUP * rows
    line_rows = FRAMES * rows
    bf16 = jnp.bfloat16
    smem = pl.BlockSpec(memory_space=pltpu.SMEM)
    vmem = pl.BlockSpec(memory_space=pltpu.VMEM)
    anywhere = pl.BlockSpec(memory_space=pl.ANY)
    packed, place, sorted_bits, logit_scale, value_factor = pl.pallas_call(
        pack,
        out_shape=(
            jax.ShapeDtypeStruct((heads, rows, 3 * WIDTH), bf16),
            jax.ShapeDtypeStruct((heads,), jnp.int32),
            jax.ShapeDtypeStruct((heads, blocks), jnp.int32),
            jax.ShapeDtypeStruct((heads,), jnp.float32),
            jax.ShapeDtypeStruct((heads,), jnp.float32),
        ),
        in_specs=[smem] * 4 + [vmem] * 4,
        out_specs=(vmem, smem, vmem, smem, smem),
        compiler_params=pltpu.CompilerParams(vmem_limit_bytes=40 * 1024 * 1024),
    )(
        labels,
        query_scale,
        key_scale,
        value_scale,
        bits,
        queries,
        key_vectors,
        value_vectors,
    )
    returned = pl.pallas_call(
        functools.partial(kernel, devices, ulysses),
        out_shape=jax.ShapeDtypeStruct((heads, rows, WIDTH), bf16),
        in_specs=[smem] * 3 + [anywhere],
        out_specs=anywhere,
        scratch_shapes=[
            pltpu.VMEM((share, near_rows + 2 * RIM, 3 * WIDTH), bf16),
            pltpu.VMEM((FRAMES, rows, 3 * WIDTH), bf16),
            pltpu.VMEM((line_rows + 2 * RIM, 3 * WIDTH), bf16),
            pltpu.VMEM((share, near_rows, WIDTH), bf16),
            pltpu.VMEM((line_rows, WIDTH), bf16),
            pltpu.VMEM((FRAMES, rows, WIDTH), bf16),
            pltpu.VMEM((16 * FRAMES, 16 * FRAMES), bf16),
            pltpu.SemaphoreType.DMA((GROUP,)),
            pltpu.SemaphoreType.DMA((GROUP,)),
            pltpu.SemaphoreType.DMA((FRAMES,)),
            pltpu.SemaphoreType.DMA((FRAMES,)),
            pltpu.SemaphoreType.DMA((4,)),
            pltpu.SemaphoreType.DMA((4,)),
            pltpu.SemaphoreType.DMA((4,)),
            pltpu.SemaphoreType.DMA((GROUP,)),
            pltpu.SemaphoreType.DMA((GROUP,)),
            pltpu.SemaphoreType.DMA((FRAMES,)),
            pltpu.SemaphoreType.DMA((FRAMES,)),
        ],
        compiler_params=pltpu.CompilerParams(
            collective_id=0, has_side_effects=True, vmem_limit_bytes=40 * 1024 * 1024
        ),
        cost_estimate=pl.CostEstimate(
            flops=10**9, bytes_accessed=4 * rows * width * 2, transcendentals=10**6
        ),
    )(sorted_bits, logit_scale, value_factor, packed)
    return pl.pallas_call(
        unpack,
        out_shape=jax.ShapeDtypeStruct((rows, width), bf16),
        in_specs=[smem, vmem],
        out_specs=vmem,
    )(place, returned)


def solution(mesh):
    tokens = P(("context", "ulysses"), None)
    devices = mesh.shape["ulysses"] * mesh.shape["context"]
    return jax.shard_map(
        functools.partial(shards, devices),
        mesh=mesh,
        in_specs=(tokens, tokens, tokens, P(), P(), P(), P(), P(), P()),
        out_specs=tokens,
        check_vma=False,
    )
```

time: 602 us -> 72.3 us (0.12)
  local copies, waits for them, and re-layouts: 197 us -> 7.63 us
  loops' own time: 117 us -> 0 us
  waiting for transfers between devices: 95.5 us -> 0 us
  blocking collectives: 81.3 us -> 0 us
  Pallas kernels: 0 us -> 62.7 us
  starting transfers between devices: 41 us -> 0 us
  other arithmetic: 39.6 us -> 0.93 us
  matrix products: 23.7 us -> 0 us
    another operation x1 -> x0, loops' own time: 117 us -> none  [attend_heads(): result = lax.map(one_head, jnp.arange(heads_here, dtype=jnp.int32))]
    dynamic_slice x160 -> x0, local copies, waits for them, and re-layouts: 99.8 us -> none  [the longest x20 19.5 us: one_head(): lax.dynamic_index_in_dim(extended, head_index, 1, keepdims=False)]
    all_to_all x6 -> x0, waiting for transfers between devices: 95.5 us -> none  [the longest x1 22.2 us: shards(): lax.all_to_all(into_pieces(frame_values, context), 'context', split_axis=...]
    all_to_all x2 -> x0, blocking collectives: 81.3 us -> none  [the longest x1 63.1 us: shards(): lax.all_to_all(out_of_lines(outputs, context, spans), 'context', split_ax...]
    pallas_call x0 -> x3, Pallas kernels: none -> 62.7 us  [the longest x1 57.9 us: shards(): pl.pallas_call(functools.partial(kernel, devices, ulysses), out_shape=jax...]
    gather x84 -> x0, local copies, waits for them, and re-layouts: 50.5 us -> none  [the longest x20 12.7 us: one_head(): jnp.take(lax.dynamic_index_in_dim(counts, head, 0, keepdims=False), globa...]
    all_to_all x6 -> x0, starting transfers between devices: 32.8 us -> none  [the longest x1 7.53 us: shards(): lax.all_to_all(into_pieces(frame_queries, context), 'context', split_axis...]
    dot_general x40 -> x0, matrix products: 23.7 us -> none  [the longest x20 18.5 us: one_head(): jnp.einsum('fac,foc->fao', query_tiles, collected_keys, preferred_element...]
  transfers between devices with their start and end apart: 10 -> 0, of which waited for: 6 -> 0; matrix products, arithmetic and copies ran while one was open for 5% -> 0% of each run, Pallas kernels for 0% -> 0%
where the time goes in v1:
time: 72.3 us; the launch traced here: 71.3 us
  Pallas kernels  62.7 us (87%)
  local copies, waits for them, and re-layouts  7.63 us (11%)
  other arithmetic  0.93 us (1%)
    pallas_call x1, Pallas kernels, shards(): pl.pallas_call(functools.partial(kernel, devices, ulysses), out_shape=jax...  57.9 us
    unnamed x18, local copies, waits for them, and re-layouts  7.63 us
    pallas_call x1, Pallas kernels, shards(): pl.pallas_call(unpack, out_shape=jax.ShapeDtypeStruct((rows, width), bf16...  2.66 us
    pallas_call x1, Pallas kernels, shards(): pl.pallas_call(pack, out_shape=(jax.ShapeDtypeStruct((heads, rows, 3 * WI...  2.13 us

profile of v1, /device:TPU:0, one launch (start us, length us, event | category | flops | bytes accessed | tf_op | source)
XLA Modules:
  0.0 71.3 jit_solution(12944575977312283968)
XLA Ops:
  0.0 0.9 %select_reduce_fusion.bits = s32[40,48]{1,0:T(8,128)S(1)} fusion(s32[40,48,5]{1,0,2:T(8,128)} %param.13, s32[40,48]{1,0:T(8,128)} %param.14), kind=kLoop, calls=%fused_computation | loop fusion | flops 55680 | bytes 53760 | tf_op jit(solution)/shard_map/reduce_sum | solution.py:417
  0.9 0.0 copy-start.1
  0.9 1.2 %copy-done.1 = bf16[96,5120]{1,0:T(8,128)(2,1)S(1)} copy-done((bf16[96,5120]{1,0:T(8,128)(2,1)S(1)}, bf16[96,5120]{1,0:T(8,128)(2,1)}, u32[]{:S(2)}) %copy-start.1) | copy-done | bytes 983064
  2.1 0.0 copy-start.2
  2.1 1.2 %copy-done.2 = bf16[96,5120]{1,0:T(8,128)(2,1)S(1)} copy-done((bf16[96,5120]{1,0:T(8,128)(2,1)S(1)}, bf16[96,5120]{1,0:T(8,128)(2,1)}, u32[]{:S(2)}) %copy-start.2) | copy-done | bytes 983064
  3.3 0.0 copy-start.3
  3.3 1.2 %copy-done.3 = bf16[96,5120]{1,0:T(8,128)(2,1)S(1)} copy-done((bf16[96,5120]{1,0:T(8,128)(2,1)S(1)}, bf16[96,5120]{1,0:T(8,128)(2,1)}, u32[]{:S(2)}) %copy-start.3) | copy-done | bytes 983064
  4.5 0.0 copy-start.4
  4.5 0.7 copy-done.4
  5.2 0.0 copy-start.5
  5.2 0.7 copy-done.5
  5.8 0.0 copy-start.6
  5.9 0.7 copy-done.6
  6.5 0.0 copy-start.7
  6.5 0.7 copy-done.7
  7.2 2.1 %shard_map.91 = (bf16[40,96,384]{2,1,0:T(8,128)(2,1)S(1)}, s32[40]{0:T(128)S(1)}, s32[40,48]{1,0:T(8,128)S(1)}, f32[40]{0:T(128)S(1)}, f32[40]{0:T(128)S(1)}) custom-call(s32[40]{0:T(128)S(1)} %copy-done.4, f32[40]{0:T(128)S(1)} %copy-done.5, f32[40]{0:T(128)S(1)} %copy-done.6, f32[40]{0:T(128)S(1)} %copy-done.7, s32[40,48]{1,0:T(8,128)S(1)} %select_reduce_fusion.bits, ...), custom_call_target="tpu_custom_call" | custom-call | tf_op jit(solution)/shard_map/pallas_call | solution.py:427
  9.3 0.0 copy-start.8
  9.3 0.5 copy-done.8
  9.8 57.9 %shard_map.92.returned = bf16[40,96,128]{2,1,0:T(8,128)(2,1)S(1)} custom-call(s32[40,48]{1,0:T(8,128)S(1)} %get-tuple-element.11.bits, f32[40]{0:T(128)S(1)} %get-tuple-element.12.logit_scale, f32[40]{0:T(128)S(1)} %get-tuple-element.13.value_scale, bf16[40,96,384]{2,1,0:T(8,128)(2,1)S(1)} %get-tuple-element.14.packed), custom_call_target="tpu_custom_call" | custom-call | flops 1000000000 | bytes 3932160 | tf_op jit(solution)/shard_map/pallas_call | solution.py:449
  67.7 0.0 copy-start
  67.7 0.9 %copy-done = bf16[40,96,128]{2,1,0:T(8,128)(2,1)} copy-done((bf16[40,96,128]{2,1,0:T(8,128)(2,1)}, bf16[40,96,128]{2,1,0:T(8,128)(2,1)S(1)}, u32[]{:S(2)}) %copy-start) | copy-done | bytes 983064
  68.6 2.7 %shard_map.93 = bf16[96,5120]{1,0:T(8,128)(2,1)} custom-call(s32[40]{0:T(128)} %copy-done.8, bf16[40,96,128]{2,1,0:T(8,128)(2,1)} %copy-done), custom_call_target="tpu_custom_call" | custom-call | tf_op jit(solution)/shard_map/pallas_call | solution.py:481
Async XLA Ops:
  0.9 1.2 %copy-start.1 = (bf16[96,5120]{1,0:T(8,128)(2,1)S(1)}, bf16[96,5120]{1,0:T(8,128)(2,1)}, u32[]{:S(2)}) copy-start(bf16[96,5120]{1,0:T(8,128)(2,1)} %q_ref.1) | copy-start | bytes 2949124
  2.1 1.2 %copy-start.2 = (bf16[96,5120]{1,0:T(8,128)(2,1)S(1)}, bf16[96,5120]{1,0:T(8,128)(2,1)}, u32[]{:S(2)}) copy-start(bf16[96,5120]{1,0:T(8,128)(2,1)} %k_ref.1) | copy-start | bytes 2949124
  3.3 1.2 %copy-start.3 = (bf16[96,5120]{1,0:T(8,128)(2,1)S(1)}, bf16[96,5120]{1,0:T(8,128)(2,1)}, u32[]{:S(2)}) copy-start(bf16[96,5120]{1,0:T(8,128)(2,1)} %v_ref.1) | copy-start | bytes 2949124
  4.5 0.7 copy-start.4
  5.2 0.7 copy-start.5
  5.8 0.7 copy-start.6
  6.5 0.7 copy-start.7
  9.3 0.5 copy-start.8
  67.7 0.9 %copy-start = (bf16[40,96,128]{2,1,0:T(8,128)(2,1)}, bf16[40,96,128]{2,1,0:T(8,128)(2,1)S(1)}, u32[]{:S(2)}) copy-start(bf16[40,96,128]{2,1,0:T(8,128)(2,1)S(1)} %shard_map.92.returned) | copy-start | bytes 2949124

commit v2 on v1

--- a/solution.py
+++ b/solution.py
@@ -20,56 +20,112 @@
 MASKED = -1e30
 
 
+def slot_of(labels, head, spatial):
+    temporal = labels[head]
+    slot = jnp.where(temporal == 1, labels.shape[0] - TEMPORAL + head - spatial, spatial)
+    return slot, spatial + 1 - temporal
+
+
 def pack(
+    labels_in,
+    query_scale_in,
+    key_scale_in,
+    value_scale_in,
+    lists_in,
+    counts_in,
+    q_in,
+    k_in,
+    v_in,
+    packed,
+    table,
     labels,
     query_scale,
     key_scale,
     value_scale,
+    lists,
+    counts,
     bits,
-    q_ref,
-    k_ref,
-    v_ref,
-    packed,
-    place,
-    sorted_bits,
-    logit_scale,
-    value_factor,
+    sems,
+    packed_sem,
 ):
-    heads = labels.shape[0]
-
-    def one(head, spatial):
-        temporal = labels[head]
-        slot = jnp.where(temporal == 1, heads - TEMPORAL + head - spatial, spatial)
-        place[head] = slot
-        logit_scale[slot] = query_scale[head] * key_scale[head] * (1.0 / math.sqrt(WIDTH))
-        value_factor[slot] = value_scale[head]
-        sorted_bits[pl.ds(slot, 1), :] = bits[pl.ds(head, 1), :]
+    heads = labels_in.shape[0]
+    small = [
+        pltpu.make_async_copy(source, target, sems.at[i])
+        for i, (source, target) in enumerate(
+            (
+                (labels_in, labels),
+                (query_scale_in, query_scale),
+                (key_scale_in, key_scale),
+                (value_scale_in, value_scale),
+                (lists_in, lists),
+                (counts_in, counts),
+            )
+        )
+    ]
+    for copy in small:
+        copy.start()
+    small[0].wait()
+
+    def move(head, spatial):
+        slot, after = slot_of(labels, head, spatial)
         columns = pl.ds(pl.multiple_of(head * WIDTH, WIDTH), WIDTH)
-        packed[slot, :, 0:WIDTH] = q_ref[:, columns]
-        packed[slot, :, WIDTH : 2 * WIDTH] = k_ref[:, columns]
-        packed[slot, :, 2 * WIDTH : 3 * WIDTH] = v_ref[:, columns]
-        return spatial + 1 - temporal
-
-    lax.fori_loop(0, heads, one, 0)
-
-
-def unpack(place, returned, out_ref):
-    def one(head, carry):
+        for i, source in enumerate((q_in, k_in, v_in)):
+            pltpu.make_async_copy(
+                source.at[:, columns],
+                packed.at[slot, :, pl.ds(i * WIDTH, WIDTH)],
+                packed_sem,
+            ).start()
+        return after
+
+    lax.fori_loop(0, heads, move, 0, unroll=4)
+    for copy in small[1:]:
+        copy.wait()
+
+    query_ids = lax.broadcasted_iota(jnp.int32, counts.shape, 1)
+    total = jnp.zeros(counts.shape, jnp.int32)
+    for j in range(lists.shape[0]):
+        offset = lists[j] - query_ids + MARGIN
+        total += jnp.where(counts[...] > j, jnp.left_shift(jnp.ones_like(offset), offset), 0)
+    bits[:, 0 : counts.shape[1]] = total.astype(jnp.float32)
+    lane = lax.broadcasted_iota(jnp.int32, (1, table.shape[1]), 1)
+
+    def sort(head, spatial):
+        slot, after = slot_of(labels, head, spatial)
+        scale = query_scale[head] * key_scale[head] * (1.0 / math.sqrt(WIDTH))
+        row = pl.ds(slot, 1)
+        table[row, :] = jnp.where(
+            lane < counts.shape[1],
+            bits[pl.ds(head, 1), :],
+            jnp.where(lane == table.shape[1] - WIDTH, scale, value_scale[head]),
+        )
+        return after
+
+    lax.fori_loop(0, heads, sort, 0)
+    pltpu.make_async_copy(packed, packed, packed_sem).wait()
+
+
+def unpack(labels_in, returned, out, labels, sem, out_sem):
+    copy = pltpu.make_async_copy(labels_in, labels, sem)
+    copy.start()
+    copy.wait()
+
+    def move(head, spatial):
+        slot, after = slot_of(labels, head, spatial)
         columns = pl.ds(pl.multiple_of(head * WIDTH, WIDTH), WIDTH)
-        out_ref[:, columns] = returned[place[head]]
-        return carry
-
-    lax.fori_loop(0, place.shape[0], one, 0)
+        pltpu.make_async_copy(returned.at[slot], out.at[:, columns], out_sem).start()
+        return after
+
+    lax.fori_loop(0, labels_in.shape[0], move, 0, unroll=4)
+    pltpu.make_async_copy(out, out, out_sem).wait()
 
 
 def kernel(
     devices,
     ulysses,
-    bits,
-    logit_scale,
-    value_scale,
+    table_in,
     packed,
     returned,
+    table,
     near,
     frames,
     lines,
@@ -88,6 +144,7 @@
     near_back_recv,
     far_back_send,
     far_back_recv,
+    small_sem,
 ):
     heads, rows = packed.shape[:2]
     spatial = heads - TEMPORAL
@@ -124,6 +181,10 @@
     line_upper = chunk < per_frame - 1
     mesh_id = pl.DeviceIdType.MESH
 
+    table_copy = pltpu.make_async_copy(table_in, table, small_sem)
+    table_copy.start()
+    logit_at = table.shape[1] - WIDTH
+
     barrier = pltpu.get_barrier_semaphore()
 
     def greet(index):
@@ -158,10 +219,10 @@
             device_id_type=mesh_id,
         )
 
+    for step in range(1, GROUP):
+        near_copy(near_peer(step), slot).start()
     for step in range(1, FRAMES):
         far_copy(far_peer(step), frame).start()
-        if step < GROUP:
-            near_copy(near_peer(step), slot).start()
     own_near = pltpu.make_async_copy(
         packed.at[pl.ds(share * slot, share)],
         near.at[:, pl.ds(RIM + rows * slot, rows), :],
@@ -234,8 +295,8 @@
     key_bit = jnp.left_shift(jnp.ones_like(key_block), key_block)
 
     def attend(queries, keys, values, head, block):
-        lower = jnp.where((key_bit & bits[head, block]) != 0, 0.0, MASKED)
-        upper = jnp.where((key_bit & (bits[head, block + 1] * 2)) != 0, 0.0, MASKED)
+        lower = jnp.where((key_bit & table[head, block].astype(jnp.int32)) != 0, 0.0, MASKED)
+        upper = jnp.where((key_bit & (table[head, block + 1].astype(jnp.int32) * 2)) != 0, 0.0, MASKED)
         bias = jnp.concatenate(
             [
                 jnp.broadcast_to(lower, (BLOCK, WINDOW)),
@@ -246,14 +307,14 @@
         score = lax.dot_general(
             queries, keys, (((1,), (1,)), ((), ())), preferred_element_type=jnp.float32
         )
-        score = score * logit_scale[head] + bias
+        score = score * table[head, logit_at] + bias
         peak = jnp.max(score, axis=-1, keepdims=True)
         weight = jnp.exp(score - peak)
         total = jnp.sum(weight, axis=-1, keepdims=True)
         mixed = jnp.dot(
             weight.astype(jnp.bfloat16), values, preferred_element_type=jnp.float32
         )
-        return (mixed * (value_scale[head] / total)).astype(jnp.bfloat16)
+        return (mixed * (table[head, logit_at + 1] / total)).astype(jnp.bfloat16)
 
     def near_pair(i, pair):
         start = pl.multiple_of(pair * PAIR, PAIR)
@@ -281,6 +342,7 @@
     for step in range(1, GROUP):
         near_copy(near_peer(step), near_peer(step)).wait_recv()
     own_near.wait()
+    table_copy.wait()
     send_rim(0)
     send_rim(1)
 
@@ -412,36 +474,41 @@
     share = spatial // GROUP
     ulysses = lax.axis_size("ulysses")
 
-    entries = jnp.arange(block_lists.shape[2], dtype=jnp.int32)
-    offsets = block_lists - jnp.arange(blocks, dtype=jnp.int32)[None, :, None] + MARGIN
-    bits = jnp.sum(
-        jnp.where(entries < counts[:, :, None], jnp.left_shift(1, offsets), 0), axis=2
-    ).astype(jnp.int32)
-
     near_rows = GROUP * rows
     line_rows = FRAMES * rows
     bf16 = jnp.bfloat16
-    smem = pl.BlockSpec(memory_space=pltpu.SMEM)
     vmem = pl.BlockSpec(memory_space=pltpu.VMEM)
     anywhere = pl.BlockSpec(memory_space=pl.ANY)
-    packed, place, sorted_bits, logit_scale, value_factor = pl.pallas_call(
+    hbm = pl.BlockSpec(memory_space=pltpu.HBM)
+    lists = jnp.transpose(block_lists, (2, 0, 1))
+    table_width = -(-blocks // WIDTH) * WIDTH + WIDTH
+    packed, table = pl.pallas_call(
         pack,
         out_shape=(
             jax.ShapeDtypeStruct((heads, rows, 3 * WIDTH), bf16),
-            jax.ShapeDtypeStruct((heads,), jnp.int32),
-            jax.ShapeDtypeStruct((heads, blocks), jnp.int32),
-            jax.ShapeDtypeStruct((heads,), jnp.float32),
-            jax.ShapeDtypeStruct((heads,), jnp.float32),
+            jax.ShapeDtypeStruct((heads, table_width), jnp.float32),
         ),
-        in_specs=[smem] * 4 + [vmem] * 4,
-        out_specs=(vmem, smem, vmem, smem, smem),
-        compiler_params=pltpu.CompilerParams(vmem_limit_bytes=40 * 1024 * 1024),
+        in_specs=[hbm] * 9,
+        out_specs=(vmem, vmem),
+        scratch_shapes=[
+            pltpu.SMEM((heads,), jnp.int32),
+            pltpu.SMEM((heads,), jnp.float32),
+            pltpu.SMEM((heads,), jnp.float32),
+            pltpu.SMEM((heads,), jnp.float32),
+            pltpu.VMEM(lists.shape, jnp.int32),
+            pltpu.VMEM((heads, blocks), jnp.int32),
+            pltpu.VMEM((heads, table_width), jnp.float32),
+            pltpu.SemaphoreType.DMA((6,)),
+            pltpu.SemaphoreType.DMA,
+        ],
+        compiler_params=pltpu.CompilerParams(vmem_limit_bytes=60 * 1024 * 1024),
     )(
         labels,
         query_scale,
         key_scale,
         value_scale,
-        bits,
+        lists,
+        counts,
         queries,
         key_vectors,
         value_vectors,
@@ -449,9 +516,10 @@
     returned = pl.pallas_call(
         functools.partial(kernel, devices, ulysses),
         out_shape=jax.ShapeDtypeStruct((heads, rows, WIDTH), bf16),
-        in_specs=[smem] * 3 + [anywhere],
+        in_specs=[anywhere] * 2,
         out_specs=anywhere,
         scratch_shapes=[
+            pltpu.SMEM((heads, table_width), jnp.float32),
             pltpu.VMEM((share, near_rows + 2 * RIM, 3 * WIDTH), bf16),
             pltpu.VMEM((FRAMES, rows, 3 * WIDTH), bf16),
             pltpu.VMEM((line_rows + 2 * RIM, 3 * WIDTH), bf16),
@@ -470,20 +538,27 @@
             pltpu.SemaphoreType.DMA((GROUP,)),
             pltpu.SemaphoreType.DMA((FRAMES,)),
             pltpu.SemaphoreType.DMA((FRAMES,)),
+            pltpu.SemaphoreType.DMA,
         ],
         compiler_params=pltpu.CompilerParams(
-            collective_id=0, has_side_effects=True, vmem_limit_bytes=40 * 1024 * 1024
+            collective_id=0, has_side_effects=True, vmem_limit_bytes=60 * 1024 * 1024
         ),
         cost_estimate=pl.CostEstimate(
             flops=10**9, bytes_accessed=4 * rows * width * 2, transcendentals=10**6
         ),
-    )(sorted_bits, logit_scale, value_factor, packed)
+    )(table, packed)
     return pl.pallas_call(
         unpack,
         out_shape=jax.ShapeDtypeStruct((rows, width), bf16),
-        in_specs=[smem, vmem],
-        out_specs=vmem,
-    )(place, returned)
+        in_specs=[hbm, anywhere],
+        out_specs=hbm,
+        compiler_params=pltpu.CompilerParams(vmem_limit_bytes=8 * 1024 * 1024),
+        scratch_shapes=[
+            pltpu.SMEM((heads,), jnp.int32),
+            pltpu.SemaphoreType.DMA,
+            pltpu.SemaphoreType.DMA,
+        ],
+    )(labels, returned)
 
 
 def solution(mesh):

time: 72.3 us -> 64.2 us (0.89)
  local copies, waits for them, and re-layouts: 7.63 us -> 1.2 us
  other arithmetic: 0.93 us -> 0 us
    unnamed x18 -> x4, local copies, waits for them, and re-layouts: 7.63 us -> 1.2 us
    pallas_call x1, Pallas kernels: 2.13 us -> 4.4 us  [shards(): pl.pallas_call(pack, out_shape=(jax.ShapeDtypeStruct((heads, rows, 3 * WI...]
    pallas_call x1, Pallas kernels: 57.9 us -> 56.5 us  [shards(): pl.pallas_call(functools.partial(kernel, devices, ulysses), out_shape=jax...]
    pallas_call x1, Pallas kernels: 2.66 us -> 1.48 us  [shards(): pl.pallas_call(unpack, out_shape=jax.ShapeDtypeStruct((rows, width), bf16...]
    reduce_sum x1 -> x0, other arithmetic: 0.93 us -> none  [shards(): jnp.sum(jnp.where(entries < counts[:, :, None], jnp.left_shift(1, offsets...]
where the time goes in v2:
time: 64.2 us; the launch traced here: 63.6 us
  Pallas kernels  62.4 us (97%)
  local copies, waits for them, and re-layouts  1.2 us (2%)
    pallas_call x1, Pallas kernels, shards(): pl.pallas_call(functools.partial(kernel, devices, ulysses), out_shape=jax...  56.5 us
    pallas_call x1, Pallas kernels, shards(): pl.pallas_call(pack, out_shape=(jax.ShapeDtypeStruct((heads, rows, 3 * WI...  4.4 us
    pallas_call x1, Pallas kernels, shards(): pl.pallas_call(unpack, out_shape=jax.ShapeDtypeStruct((rows, width), bf16...  1.48 us

profile of v2, /device:TPU:0, one launch (start us, length us, event | category | flops | bytes accessed | tf_op | source)
XLA Modules:
  0.0 63.6 jit_solution(1925413897959262943)
XLA Ops:
  0.0 0.0 copy-start.1
  0.0 4.4 %shard_map.91 = (bf16[40,96,384]{2,1,0:T(8,128)(2,1)}, f32[40,256]{1,0:T(8,128)}) custom-call(s32[40]{0:T(128)} %labels_in.3, f32[40]{0:T(128)} %query_scale_in.1, f32[40]{0:T(128)} %key_scale_in.1, f32[40]{0:T(128)} %value_scale_in.1, s32[5,40,48]{2,1,0:T(8,128)} %bitcast.1, s32[40,48]{1,0:T(8,128)} %counts_in.1, bf16[96,5120]{1,0:T(8,128)(2,1)} %q_in.1, ...), custom_call_target="tpu_custom_call" | custom-call | tf_op jit(solution)/shard_map/pallas_call | solution.py:485
  4.4 56.5 %shard_map.92.returned = bf16[40,96,128]{2,1,0:T(8,128)(2,1)} custom-call(f32[40,256]{1,0:T(8,128)} %get-tuple-element.7.table_in, bf16[40,96,384]{2,1,0:T(8,128)(2,1)} %get-tuple-element.8.packed), custom_call_target="tpu_custom_call" | custom-call | flops 1000000000 | bytes 3932160 | tf_op jit(solution)/shard_map/pallas_call | solution.py:516
  60.9 0.0 copy-done.1
  60.9 0.0 copy-start
  60.9 1.2 %copy-done = bf16[40,96,128]{2,1,0:T(8,128)(2,1)S(1)} copy-done((bf16[40,96,128]{2,1,0:T(8,128)(2,1)S(1)}, bf16[40,96,128]{2,1,0:T(8,128)(2,1)}, u32[]{:S(2)}) %copy-start) | copy-done | bytes 983064
  62.1 1.5 %shard_map.93 = bf16[96,5120]{1,0:T(8,128)(2,1)} custom-call(s32[40]{0:T(128)S(1)} %copy-done.1, bf16[40,96,128]{2,1,0:T(8,128)(2,1)S(1)} %copy-done), custom_call_target="tpu_custom_call" | custom-call | tf_op jit(solution)/shard_map/pallas_call | solution.py:550
Async XLA Ops:
  0.0 60.9 %copy-start.1 = (s32[40]{0:T(128)S(1)}, s32[40]{0:T(128)}, u32[]{:S(2)}) copy-start(s32[40]{0:T(128)} %labels_in.3) | copy-start | bytes 484
  60.9 1.2 %copy-start = (bf16[40,96,128]{2,1,0:T(8,128)(2,1)S(1)}, bf16[40,96,128]{2,1,0:T(8,128)(2,1)}, u32[]{:S(2)}) copy-start(bf16[40,96,128]{2,1,0:T(8,128)(2,1)} %shard_map.92.returned) | copy-start | bytes 2949124
